TPU v7x, 32 devices: a whole 2x2x4 slice. The times are simulated.
32 devices in a mesh: chan: 8 (over z, core), grp: 4 (over y, x).
Axes of the slice: x: 2, y: 2, z: 4, core: 2. Of those that a mesh axis runs over, the one named last changes fastest.
Arguments:
- residual: bfloat16 [128, 4096], P('grp', 'chan'), may hold values from -6 to 6
- conv_input: bfloat16 [128, 8192], P('grp', 'chan'), may hold values from -6 to 6
- gate_input: bfloat16 [128, 8192], P('grp', 'chan'), may hold values from -6 to 6
- conv_state: bfloat16 [128, 3, 8192], P('grp', None, 'chan'), may hold values from -6 to 6
- conv_weight: float32 [4, 8192], P(None, 'chan'), may hold values from -3 to 3
- conv_bias: float32 [8192], P('chan'), may hold values from -1 to 1
- state_proj: bfloat16 [8192, 288], P('chan'), may hold values from -0.0625 to 0.0625
- step_proj: bfloat16 [256, 8192], P(None, 'chan'), may hold values from -0.375 to 0.375
- step_bias: float32 [8192], P('chan'), may hold values from -5 to -1
- decay_rate: float32 [16, 8192], P(None, 'chan'), may hold values from 1 to 16
- skip_gain: float32 [8192], P('chan'), may hold values from 0.5 to 1.5
- ssm_state: float32 [128, 16, 8192], P('grp', None, 'chan'), may hold values from -6 to 6
- out_proj: bfloat16 [8192, 4096], P('chan'), may hold values from -0.0625 to 0.0625
- router: bfloat16 [4096, 4], P('chan'), may hold values from -0.09375 to 0.09375
- expert_ids: int32 [128, 2], P('grp'), may hold values from 0 to 3, all different within a row; in each aligned block of 32 rows (0 to 31, 32 to 63, ...) at most 24 rows name the same one
- expert_gate: bfloat16 [4, 4096, 16384], P('grp', None, 'chan'), may hold values from -0.09375 to 0.09375
- expert_up: bfloat16 [4, 4096, 16384], P('grp', None, 'chan'), may hold values from -0.09375 to 0.09375
- expert_down: bfloat16 [4, 16384, 4096], P('grp', 'chan'), may hold values from -0.046875 to 0.046875
Outputs:
- layer_out: bfloat16 [128, 4096], P('grp', 'chan')
- new_state: float32 [128, 16, 8192], P('grp', None, 'chan')
Inputs may be any that keep to these rules, and one draw needn't show every extreme that they name: `expert_ids`: each request names two different experts; among the 32 requests of one group no expert is named more than 24 times, and in some group some expert is named exactly 24 times.
All inputs are finite; a program needn't handle non-finite values.
Results may differ from a plain program's by a relative error of at most 0.0056.
The roundings to bfloat16 on the way count: a program that leaves them out, or rounds other values in their place, can miss the bound.
Values may be sent and summed in bfloat16 or wider, within the bound.
A program may use at most 192 MiB of HBM per device.

v0:
```python
import jax
import jax.numpy as jnp
from jax import lax
from jax.sharding import PartitionSpec as P

EPSILON = 1e-06


def per_device(
    residual,
    conv_input,
    gate_input,
    conv_state,
    conv_weight,
    conv_bias,
    state_proj,
    step_proj,
    step_bias,
    decay_rate,
    skip_gain,
    ssm_state,
    out_proj,
    router,
    expert_ids,
    expert_gate,
    expert_up,
    expert_down,
):
    row_count = residual.shape[0]
    part_width = residual.shape[1]
    groups = lax.axis_size("grp")
    channels = lax.axis_size("chan")
    full_width = part_width * channels
    step_rank = step_proj.shape[0]
    nstates = decay_rate.shape[0]
    capacity = 3 * row_count // 4
    experts = router.shape[1]
    sharers = groups // experts
    window = conv_state.astype(jnp.float32)
    convolved = (
        conv_weight[0] * window[:, 0]
        + conv_weight[1] * window[:, 1]
        + conv_weight[2] * window[:, 2]
        + conv_weight[3] * conv_input.astype(jnp.float32)
        + conv_bias
    )
    inner_act = jax.nn.silu(convolved).astype(jnp.bfloat16)
    projected = lax.psum(jnp.dot(inner_act, state_proj, preferred_element_type=jnp.float32), "chan")
    step_raw = projected[:, :step_rank]
    input_mix = projected[:, step_rank : step_rank + nstates]
    output_mix = projected[:, step_rank + nstates :]
    step_norm = (
        step_raw * lax.rsqrt(jnp.mean(step_raw * step_raw, axis=1, keepdims=True) + EPSILON)
    ).astype(jnp.bfloat16)
    step_size = jax.nn.softplus(
        jnp.dot(step_norm, step_proj, preferred_element_type=jnp.float32) + step_bias
    )
    inner_wide = inner_act.astype(jnp.float32)
    decay_factor = jnp.exp(-step_size[:, None, :] * decay_rate[None, :, :])
    new_state = (
        decay_factor * ssm_state + (step_size * inner_wide)[:, None, :] * input_mix[:, :, None]
    )
    readout = jnp.sum(output_mix[:, :, None] * new_state, axis=1) + skip_gain * inner_wide
    gated_out = (readout * jax.nn.silu(gate_input.astype(jnp.float32))).astype(jnp.bfloat16)
    columns = out_proj
    mixer_part = lax.psum_scatter(
        lax.dot_general(
            columns, gated_out, (((0,), (1,)), ((), ())), preferred_element_type=jnp.float32
        ),
        "chan",
        scatter_dimension=0,
        tiled=True,
    )
    hidden_mid = residual.astype(jnp.float32) + mixer_part.T
    squares = jnp.sum(hidden_mid * hidden_mid, axis=1)
    router_wide = router.astype(jnp.float32)
    sum_squares = lax.psum(squares, "chan")
    inv_rms = lax.rsqrt(sum_squares / full_width + EPSILON)
    logits = lax.psum(
        jnp.dot(hidden_mid * inv_rms[:, None], router_wide, precision=lax.Precision.HIGHEST), "chan"
    )
    normed = (hidden_mid * inv_rms[:, None]).astype(jnp.bfloat16)
    labels = jnp.arange(experts, dtype=jnp.int32)
    chosen = jnp.sum(
        logits[:, None, :] * (expert_ids[:, :, None] == labels).astype(jnp.float32), axis=2
    )
    weight_first = jax.nn.sigmoid(chosen[:, 0] - chosen[:, 1])
    weight_second = 1.0 - weight_first
    flat_ids = expert_ids.reshape(-1)
    matches = (flat_ids[:, None] == labels).astype(jnp.int32)
    position = jnp.sum((jnp.cumsum(matches, axis=0) - matches) * matches, axis=1)
    target = flat_ids * capacity + position
    placing = (jnp.arange(experts * capacity, dtype=jnp.int32)[:, None] == target[None, :]).astype(
        jnp.bfloat16
    )
    repeated = jnp.repeat(normed, 2, axis=0)
    outgoing = jnp.dot(placing, repeated, preferred_element_type=jnp.float32).astype(jnp.bfloat16)
    copies = jnp.repeat(outgoing.reshape(experts, capacity, part_width), sharers, axis=0)
    incoming = lax.all_to_all(copies, "grp", split_axis=0, concat_axis=0, tiled=True)
    portion = lax.all_gather(
        incoming.reshape(groups * capacity, part_width), "chan", axis=1, tiled=True
    )
    gate_part = expert_gate[0]
    up_part = expert_up[0]
    gate_sum = jnp.dot(portion, gate_part, preferred_element_type=jnp.float32)
    up_sum = jnp.dot(portion, up_part, preferred_element_type=jnp.float32)
    hidden = (jax.nn.silu(gate_sum) * up_sum).astype(jnp.bfloat16)
    columns = expert_down[0]
    summed = lax.psum_scatter(
        lax.dot_general(
            columns, hidden, (((0,), (1,)), ((), ())), preferred_element_type=jnp.float32
        ),
        "chan",
        scatter_dimension=0,
        tiled=True,
    )
    answer = summed.T.astype(jnp.bfloat16)
    returned = lax.all_to_all(
        answer.reshape(groups, capacity, part_width), "grp", split_axis=0, concat_axis=0, tiled=True
    )
    combined = jnp.sum(
        returned.astype(jnp.float32).reshape(experts, sharers, capacity, part_width), axis=1
    )
    answers = lax.dot_general(
        placing.astype(jnp.float32),
        combined.reshape(experts * capacity, part_width),
        (((0,), (0,)), ((), ())),
        precision=lax.Precision.HIGHEST,
        preferred_element_type=jnp.float32,
    ).reshape(row_count, 2, part_width)
    layer_out = (
        hidden_mid + weight_first[:, None] * answers[:, 0] + weight_second[:, None] * answers[:, 1]
    ).astype(jnp.bfloat16)
    return (layer_out, new_state)


def solution(mesh):
    return jax.shard_map(
        per_device,
        mesh=mesh,
        in_specs=(
            P("grp", "chan"),
            P("grp", "chan"),
            P("grp", "chan"),
            P("grp", None, "chan"),
            P(None, "chan"),
            P("chan"),
            P("chan", None),
            P(None, "chan"),
            P("chan"),
            P(None, "chan"),
            P("chan"),
            P("grp", None, "chan"),
            P("chan", None),
            P("chan", None),
            P("grp", None),
            P("grp", None, "chan"),
            P("grp", None, "chan"),
            P("grp", "chan", None),
        ),
        out_specs=(P("grp", "chan"), P("grp", None, "chan")),
        check_vma=False,
    )
```

profile of v0, /device:TPU:0, one launch (start us, length us, event | category | flops | bytes accessed | tf_op | source)
XLA Modules:
  0.0 196.5 jit_solution(4262304531958366713)
XLA Ops:
  7.2 0.9 fusion.51
  8.1 1.0 convert_element_type.51
  9.1 0.9 multiply_convert_fusion
  10.0 0.3 fusion.52
  10.3 30.7 %psum.21 = f32[32,288]{1,0:T(8,128)S(1)} all-reduce(f32[32,288]{1,0:T(8,128)S(1)} %fusion.52), channel_id=1, replica_groups=mesh['chan'=8,'grp'=4] {'chan'}, use_global_device_ids=true, to_apply=%region_0.1 | all-reduce | flops 9216 | bytes 73728 | tf_op jit(solution)/shard_map/psum | solution.py:48
  41.0 0.1 multiply_reduce_fusion.2
  41.2 1.3 fusion.49
  42.6 3.8 %multiply_reduce_fusion = (f32[32,1024]{1,0:T(8,128)S(1)}, f32[32,16,1024]{2,1,0:T(8,128)}) fusion(f32[32,16]{1,0:T(8,128)S(1)} %get-tuple-element.9, f32[32,16]{1,0:T(8,128)S(1)} %get-tuple-element.8, f32[32,1024]{1,0:T(8,128)S(1)} %get-tuple-element.7, f32[32,16,1024]{2,1,0:T(8,128)} %param.29, f32[16,1024]{1,0:T(8,128)} %param.27, ...), kind=kLoop, calls=%fused_computation.10 | loop fusion | flops 3112960 | bytes 4657152 | tf_op jit(solution)/shard_map/reduce_sum | solution.py:63
  46.3 5.8 %convolution_bitcast_fusion = f32[4096,32]{0,1:T(8,128)} fusion(bf16[1024,4096]{1,0:T(8,128)(2,1)} %param.30, f32[32,1024]{1,0:T(8,128)S(1)} %get-tuple-element.4, bf16[32,1024]{1,0:T(8,128)(2,1)S(1)} %multiply_convert_fusion, bf16[32,1024]{1,0:T(8,128)(2,1)} %param.20, f32[1024]{0:T(1024)} %param.28), kind=kOutput, calls=%fused_computation.7 | convolution fusion | flops 268763136 | bytes 9179136 | tf_op jit(solution)/shard_map/dot_general | solution.py:67
  52.2 0.1 copy.27
  52.3 0.1 reshape.78
  52.4 0.1 fusion.41
  52.5 0.1 reduce_window_sum.11
  52.6 0.2 select_reduce_fusion
  52.8 28.7 %reduce-scatter.3.cloned.1.call-done = f32[512,32]{0,1:T(8,128)} async-done(((f32[4096,32]{0,1:T(8,128)}), f32[512,32]{0,1:T(8,128)}) %reduce-scatter.3.cloned.1.call-update) | async-done | bytes 65552 | tf_op jit(solution)/shard_map/reduce_scatter | solution.py:66
  81.5 1.0 multiply_reduce_fusion.1
  82.4 13.7 %psum.22 = f32[32]{0:T(128)S(1)} all-reduce(f32[32]{0:T(128)S(1)} %multiply_reduce_fusion.1), channel_id=1, replica_groups=mesh['chan'=8,'grp'=4] {'chan'}, use_global_device_ids=true, to_apply=%region_5.6 | all-reduce | flops 32 | bytes 256 | tf_op jit(solution)/shard_map/psum | solution.py:77
  96.1 0.9 multiply_convert_fusion.1
  97.1 0.1 convolution_convert_fusion
  97.3 8.6 %all_to_all.10 = bf16[4,24,512]{2,1,0:T(8,128)(2,1)S(1)} all-to-all(bf16[4,24,512]{2,1,0:T(8,128)(2,1)S(1)} %bitcast.102), channel_id=1, replica_groups=mesh['chan'=8,'grp'=4] {'grp'}, dimensions={0} | all-to-all | bytes 196608 | tf_op jit(solution)/shard_map/all_to_all | solution.py:99
  105.9 15.8 %all_gather.3 = bf16[96,4096]{1,0:T(8,128)(2,1)S(1)} all-gather(bf16[96,512]{1,0:T(8,128)(2,1)S(1)} %bitcast.103), channel_id=1, replica_groups=mesh['chan'=8,'grp'=4] {'chan'}, dimensions={1}, use_global_device_ids=true | all-gather | bytes 884736 | tf_op jit(solution)/shard_map/all_gather | solution.py:100
  121.7 8.5 %fusion.4 = f32[96,2048]{1,0:T(8,128)S(1)} fusion(bf16[96,4096]{1,0:T(8,128)(2,1)S(1)} %all_gather.3, bf16[1,4096,2048]{2,1,0:T(8,128)(2,1)} %param.33), kind=kOutput, calls=%fused_computation.4 | convolution fusion | flops 1610612736 | bytes 18350080 | tf_op jit(solution)/shard_map/dot_general | solution.py:105
  130.3 17.2 %fusion.6 = f32[4096,96]{0,1:T(8,128)} fusion(bf16[1,2048,4096]{2,1,0:T(8,128)(2,1)} %param.35, bf16[96,4096]{1,0:T(8,128)(2,1)S(1)} %all_gather.3, bf16[1,4096,2048]{2,1,0:T(8,128)(2,1)} %param.34, f32[96,2048]{1,0:T(8,128)S(1)} %fusion.4), kind=kOutput, calls=%fused_computation.6 | convolution fusion | flops 3222405120 | bytes 36700160 | tf_op jit(solution)/shard_map/dot_general | solution.py:110
  147.5 0.1 iota_compare_fusion.3
  147.7 0.2 fusion.39
  147.9 14.4 %psum.23 = f32[32,4]{0,1:T(4,128)S(1)} all-reduce(f32[32,4]{0,1:T(4,128)S(1)} %fusion.39), channel_id=1, replica_groups=mesh['chan'=8,'grp'=4] {'chan'}, use_global_device_ids=true, to_apply=%region_6.7 | all-reduce | flops 128 | bytes 1024 | tf_op jit(solution)/shard_map/psum | solution.py:79
  162.3 16.7 %reduce-scatter.5.cloned.1.call-done = f32[512,96]{0,1:T(8,128)} async-done(((f32[4096,96]{0,1:T(8,128)}), f32[512,96]{0,1:T(8,128)}) %reduce-scatter.5.cloned.1.call-update) | async-done | bytes 196624 | tf_op jit(solution)/shard_map/reduce_scatter | solution.py:109
  179.0 1.6 convert_element_type.62
  180.5 3.3 %all-to-all-start.1 = ((bf16[4,24,512]{2,1,0:T(8,128)(2,1)}), bf16[4,24,512]{2,1,0:T(8,128)(2,1)S(1)}, u32[]{:S(2)}, u32[]{:S(2)}) async-start(bf16[4,24,512]{2,1,0:T(8,128)(2,1)} %bitcast.17), calls=%async_computation.3 | async-start | bytes 196608 | tf_op jit(solution)/shard_map/all_to_all | solution.py:118
  183.8 4.9 %all-to-all-done.1 = bf16[4,24,512]{2,1,0:T(8,128)(2,1)S(1)} async-done(((bf16[4,24,512]{2,1,0:T(8,128)(2,1)}), bf16[4,24,512]{2,1,0:T(8,128)(2,1)S(1)}, u32[]{:S(2)}, u32[]{:S(2)}) %all-to-all-start.1) | async-done | bytes 98336 | tf_op jit(solution)/shard_map/all_to_all | solution.py:118
  188.8 0.1 fusion.43
  188.9 0.7 fusion.34
  (25 shorter events, 0.4 us)
Async XLA Ops:
  7.2 2.8 %copy-start = (bf16[1024,288]{0,1:T(8,128)(2,1)S(1)}, bf16[1024,288]{0,1:T(8,128)(2,1)}, u32[]{:S(2)}) copy-start(bf16[1024,288]{0,1:T(8,128)(2,1)} %param.24) | copy-start | bytes 1769476
  7.2 74.3 %reduce-scatter.3.cloned.1.call-start = ((), (), s32[]{:S(2)}) async-start(), calls=%async_computation.4 | async-start | bytes 589824 | tf_op jit(solution)/shard_map/reduce_scatter | solution.py:66
  46.3 5.9 %copy-start.5 = (s32[32,2]{0,1:T(2,128)S(1)}, s32[32,2]{0,1:T(2,128)}, u32[]{:S(2)}) copy-start(s32[32,2]{0,1:T(2,128)} %param.32) | copy-start | bytes 772
  46.3 35.1 %copy-start.3 = (bf16[32,512]{1,0:T(8,128)(2,1)S(1)}, bf16[32,512]{1,0:T(8,128)(2,1)}, u32[]{:S(2)}) copy-start(bf16[32,512]{1,0:T(8,128)(2,1)} %param.18) | copy-start | bytes 98308
  52.1 126.8 %reduce-scatter.5.cloned.1.call-start = ((), (), s32[]{:S(2)}) async-start(), calls=%async_computation.5 | async-start | bytes 1769472 | tf_op jit(solution)/shard_map/reduce_scatter | solution.py:109
  130.2 17.4 %copy-start.2 = (f32[512,32]{0,1:T(8,128)S(1)}, f32[512,32]{0,1:T(8,128)}, u32[]{:S(2)}) copy-start(f32[512,32]{0,1:T(8,128)} %reduce-scatter.3.cloned.1.call-done) | copy-start | bytes 196612
  130.2 17.4 %copy-start.4 = (bf16[512,4]{0,1:T(4,128)(2,1)S(1)}, bf16[512,4]{0,1:T(4,128)(2,1)}, u32[]{:S(2)}) copy-start(bf16[512,4]{0,1:T(4,128)(2,1)} %param.31) | copy-start | bytes 12292
  130.2 59.4 %copy-start.1 = (bf16[1024,288]{0,1:T(8,128)(2,1)S(1)}, bf16[1024,288]{0,1:T(8,128)(2,1)}, u32[]{:S(2)}) copy-start(bf16[1024,288]{0,1:T(8,128)(2,1)} %param.24) | copy-start | bytes 1769476
  180.5 8.3 %all-to-all-start.1 = ((bf16[4,24,512]{2,1,0:T(8,128)(2,1)}), bf16[4,24,512]{2,1,0:T(8,128)(2,1)S(1)}, u32[]{:S(2)}, u32[]{:S(2)}) async-start(bf16[4,24,512]{2,1,0:T(8,128)(2,1)} %bitcast.17), calls=%async_computation.3 | async-start | bytes 196608 | tf_op jit(solution)/shard_map/all_to_all | solution.py:118
Sparse Core Ops, SparseCore 0:
  52.3 29.1 reduce-scatter.2
  147.6 31.2 reduce-scatter.4
where the time goes:
time: 197 us; the launch traced here: 196 us
  blocking collectives  83.2 us (42%)
  waiting for transfers between devices  50.3 us (26%)
  matrix products  33.7 us (17%)
  between operations  14.2 us (7%)
  other arithmetic  10.4 us (5%)
  starting transfers between devices  3.4 us (2%)
    psum x1, blocking collectives, per_device(): lax.psum(jnp.dot(inner_act, state_proj, preferred_element_type=jnp.float3...  30.7 us
    reduce_scatter x1, waiting for transfers between devices, per_device(): lax.psum_scatter(lax.dot_general(columns, gated_out, (((0,), (1,)), ((),...  28.7 us
    dot_general x1, matrix products, per_device(): lax.dot_general(columns, hidden, (((0,), (1,)), ((), ())), preferred_elem...  17.2 us
    reduce_scatter x1, waiting for transfers between devices, per_device(): lax.psum_scatter(lax.dot_general(columns, hidden, (((0,), (1,)), ((), ())...  16.7 us
    all_gather x1, blocking collectives, per_device(): lax.all_gather(incoming.reshape(groups * capacity, part_width), 'chan', a...  15.8 us
    psum x1, blocking collectives, per_device(): lax.psum(jnp.dot(hidden_mid * inv_rms[:, None], router_wide, precision=la...  14.4 us
    psum x1, blocking collectives, per_device(): sum_squares = lax.psum(squares, 'chan')  13.7 us
    all_to_all x1, blocking collectives, per_device(): lax.all_to_all(copies, 'grp', split_axis=0, concat_axis=0, tiled=True)  8.62 us
  transfers between devices with their start and end apart: 3, of which 3 were waited for; matrix products, arithmetic and copies ran while one was open for 0% of the time, Pallas kernels for 0%

commit v1 on v0

v1 whole, which is shorter than its diff:
```python
import functools

import jax
import jax.numpy as jnp
from jax import lax
from jax.experimental import pallas as pl
from jax.experimental.pallas import tpu as pltpu
from jax.sharding import PartitionSpec as P

EPSILON = 1e-06
F32 = jnp.float32
BF16 = jnp.bfloat16


def fused(
    chans,
    groups,
    experts,
    inner_ref,
    residual_ref,
    gate_in_ref,
    state_proj_ref,
    step_proj_ref,
    step_bias_ref,
    decay_ref,
    skip_ref,
    router_ref,
    ids_ref,
    ssm_hbm,
    out_proj_hbm,
    gate_hbm,
    up_hbm,
    down_hbm,
    layer_ref,
    state_hbm,
    w_gate,
    w_up,
    w_down,
    w_share,
    state,
    partial,
    proj_send,
    proj_recv,
    proj_all,
    proj,
    step_buf,
    drive_buf,
    read_buf,
    mix_send,
    mix_recv,
    mid_send,
    mid_recv,
    rows_x,
    stat_own,
    stat_recv,
    stat_all,
    acc_gate,
    acc_up,
    hidden,
    pair_send,
    pair_recv,
    ans_send,
    ans_recv,
    fin_send,
    fin_recv,
    local_sem,
    send_sem,
    recv_sem,
):
    me = lax.axis_index("chan")
    grp = lax.axis_index("grp")
    core = lax.rem(me, 2)
    zed = lax.div(me, 2)
    zeds = chans // 2
    partner = me + 1 - 2 * core
    sharers = groups // experts
    rows, width = residual_ref.shape
    full = width * chans
    half = full // 2
    chn = inner_ref.shape[1]
    rank = step_proj_ref.shape[0]
    nst = decay_ref.shape[0]
    hid = w_down.shape[0]
    rn = rows // chans
    allrows = rows * groups

    counters = {"local": 0, "remote": 0}

    def local(src, dst):
        k = counters["local"]
        counters["local"] += 1
        copy = pltpu.make_async_copy(src, dst, local_sem.at[k])
        copy.start()
        return copy

    def remote(src, dst, **to):
        k = counters["remote"]
        counters["remote"] += 1
        copy = pltpu.make_async_remote_copy(
            src_ref=src,
            dst_ref=dst,
            send_sem=send_sem.at[k],
            recv_sem=recv_sem.at[k],
            device_id=to,
            device_id_type=pl.DeviceIdType.MESH,
        )
        copy.start()
        sent.append(copy)
        return copy

    sent = []

    def columns(z, other):
        parity = (1 - core) if other else core
        return pl.ds(pl.multiple_of((2 * z + parity) * width, width), width)

    state_in = local(ssm_hbm, state)
    mixer_in = [
        local(
            out_proj_hbm.at[:, columns(z, p == 0)],
            w_share.at[pl.ds(p * chn, chn), pl.ds(z * width, width)],
        )
        for p in range(2)
        for z in range(zeds)
    ]
    expert_in = [[], []]
    for p in range(2):
        for src, dst in ((gate_hbm, w_gate), (up_hbm, w_up)):
            for z in range(zeds):
                expert_in[p].append(
                    local(
                        src.at[0, columns(z, p == 1), :],
                        dst.at[p, pl.ds(z * width, width), :],
                    )
                )
    down_in = [
        local(down_hbm.at[0, :, columns(z, True)], w_down.at[:, pl.ds(z * width, width)])
        for z in range(zeds)
    ]

    barrier = pltpu.get_barrier_semaphore()
    for d in range(1, chans):
        pl.semaphore_signal(
            barrier,
            inc=1,
            device_id={"chan": lax.rem(me + d, chans)},
            device_id_type=pl.DeviceIdType.MESH,
        )
    for d in range(1, groups):
        pl.semaphore_signal(
            barrier,
            inc=1,
            device_id={"grp": lax.rem(grp + d, groups)},
            device_id_type=pl.DeviceIdType.MESH,
        )

    inner = inner_ref[...]
    padded = proj.shape[1]
    partial[:, rank:] = jnp.zeros((rows, padded - rank), F32)
    partial[:, : rank + 2 * nst] = jnp.dot(
        inner, state_proj_ref[...], preferred_element_type=F32
    )
    for j in range(chans):
        proj_send[j] = partial[j * rn : (j + 1) * rn, :]
    pl.semaphore_wait(barrier, chans - 1 + groups - 1)
    arrivals = []
    for d in range(1, chans):
        to = lax.rem(me + d, chans)
        arrivals.append(remote(proj_send.at[to], proj_recv.at[d], chan=to))
    total = proj_send[me]
    for d in range(1, chans):
        arrivals[d - 1].wait_recv()
        total = total + proj_recv[d]
    proj_all[me] = total
    arrivals = []
    for d in range(1, chans):
        to = lax.rem(me + d, chans)
        arrivals.append(remote(proj_all.at[me], proj_all.at[me], chan=to))
    inner_wide = inner.astype(F32)
    gate_in = gate_in_ref[...].astype(F32)
    for copy in arrivals:
        copy.wait_recv()
    for j in range(chans):
        proj[j * rn : (j + 1) * rn, :] = proj_all[j]

    step_raw = proj[:, :rank]
    step_norm = (
        step_raw * lax.rsqrt(jnp.mean(step_raw * step_raw, axis=1, keepdims=True) + EPSILON)
    ).astype(BF16)
    logit = jnp.dot(step_norm, step_proj_ref[...], preferred_element_type=F32) + step_bias_ref[...]
    step = jnp.maximum(logit, 0.0) + jnp.log1p(jnp.exp(-jnp.abs(logit)))
    step_buf[...] = step
    drive_buf[...] = step * inner_wide
    mixing = proj[:, rank:].T
    in_mix, out_mix = mixing[:nst], mixing[nst : 2 * nst]
    request = lax.broadcasted_iota(jnp.int32, (nst, rows), 1)
    state_in.wait()

    def update(r, carry):
        mine = request == r
        mix_in = jnp.sum(jnp.where(mine, in_mix, 0.0), axis=1, keepdims=True)
        mix_out = jnp.sum(jnp.where(mine, out_mix, 0.0), axis=1, keepdims=True)
        row = pl.ds(r, 1)
        new = jnp.exp(-step_buf[row, :] * decay_ref[...]) * state[r] + drive_buf[row, :] * mix_in
        state[r] = new
        read_buf[row, :] = jnp.sum(mix_out * new, axis=0, keepdims=True)
        return carry

    lax.fori_loop(0, rows, update, 0, unroll=4)
    state_out = local(state, state_hbm)
    readout = read_buf[...] + skip_ref[...] * inner_wide
    gated = (readout * (gate_in * jax.nn.sigmoid(gate_in))).astype(BF16)

    for copy in mixer_in:
        copy.wait()
    arrivals = []
    for d in range(zeds):
        z = lax.rem(zed + d + 1, zeds)
        mix_send[d] = jnp.dot(
            gated,
            w_share[:chn, pl.ds(pl.multiple_of(z * width, width), width)],
            preferred_element_type=F32,
        ).astype(BF16)
        arrivals.append(remote(mix_send.at[d], mix_recv.at[d], chan=partner))
    crossing = []
    for d in range(zeds):
        z = lax.rem(zed + d + 1, zeds)
        mine = jnp.dot(
            gated,
            w_share[chn : 2 * chn, pl.ds(pl.multiple_of(z * width, width), width)],
            preferred_element_type=F32,
        )
        arrivals[d].wait_recv()
        mine = mine + mix_recv[d].astype(F32)
        if d < zeds - 1:
            mid_send[d] = mine.astype(BF16)
            crossing.append(remote(mid_send.at[d], mid_recv.at[d], chan=2 * z + core))
    share_in = [
        local(
            down_hbm.at[0, :, columns(z, False)],
            w_share.at[pl.ds(0, hid), pl.ds(z * width, width)],
        )
        for z in range(zeds)
    ]
    mid = residual_ref[...].astype(F32) + mine
    for d in range(zeds - 1):
        crossing[d].wait_recv()
        mid = mid + mid_recv[d].astype(F32)

    own_rows = pl.ds(pl.multiple_of(grp * rows, rows), rows)

    def cell(z):
        return rows_x.at[0, own_rows, pl.ds(pl.multiple_of(z * width, width), width)]

    rows_x[0, own_rows, pl.ds(pl.multiple_of(zed * width, width), width)] = mid.astype(BF16)
    over_z = []
    for d in range(1, zeds):
        to = lax.rem(zed + d, zeds)
        over_z.append(remote(cell(zed), cell(zed), chan=2 * to + core))
    over_grp = []
    for d in range(zeds):
        if d:
            over_z[d - 1].wait_recv()
        z = lax.rem(zed + zeds - d, zeds)
        for e in range(1, groups):
            over_grp.append(remote(cell(z), cell(z), grp=lax.rem(grp + e, groups)))
        if d == 0:
            lane = lax.broadcasted_iota(jnp.int32, (rows, 128), 1)
            squares = jnp.sum(mid * mid, axis=1, keepdims=True)
            scores = jnp.dot(
                mid,
                router_ref[...],
                precision=lax.Precision.HIGHEST,
                preferred_element_type=F32,
            )
            stat_own[...] = jnp.where(lane == experts, squares, scores)
            stats = []
            for c in range(1, chans):
                to = lax.rem(me + c, chans)
                stats.append(remote(stat_own, stat_recv.at[c], chan=to))
    summary = stat_own[...]
    for c in range(1, chans):
        stats[c - 1].wait_recv()
        summary = summary + stat_recv[c]
    stat_all[own_rows, :] = summary
    stats = []
    for e in range(1, groups):
        stats.append(
            remote(
                stat_all.at[own_rows, :],
                stat_all.at[own_rows, :],
                grp=lax.rem(grp + e, groups),
            )
        )
    for copy in over_grp:
        copy.wait_recv()
    across = remote(rows_x.at[0], rows_x.at[1], chan=partner)

    tile = min(256, hid)
    for copy in expert_in[0]:
        copy.wait()

    def first(n, carry):
        at = pl.ds(pl.multiple_of(n * tile, tile), tile)
        acc_gate[:, at] = jnp.dot(rows_x[0], w_gate[0, :, at], preferred_element_type=F32)
        acc_up[:, at] = jnp.dot(rows_x[0], w_up[0, :, at], preferred_element_type=F32)
        return carry

    lax.fori_loop(0, hid // tile, first, 0)

    scale = lax.rsqrt(summary[:, experts : experts + 1] / full + EPSILON)
    logits = summary * scale
    first_id, second_id = ids_ref[:, 0:1], ids_ref[:, 1:2]
    chosen_first = jnp.sum(jnp.where(lane == first_id, logits, 0.0), axis=1, keepdims=True)
    chosen_second = jnp.sum(jnp.where(lane == second_id, logits, 0.0), axis=1, keepdims=True)
    weight_first = jax.nn.sigmoid(chosen_first - chosen_second)
    weight_second = 1.0 - weight_first

    for copy in stats:
        copy.wait_recv()
    inv_rms = lax.rsqrt(stat_all[:, experts : experts + 1] / full + EPSILON)
    for copy in expert_in[1]:
        copy.wait()
    across.wait_recv()

    def second(n, carry):
        at = pl.ds(pl.multiple_of(n * tile, tile), tile)
        gate = acc_gate[:, at] + jnp.dot(
            rows_x[1], w_gate[1, :, at], preferred_element_type=F32
        )
        up = acc_up[:, at] + jnp.dot(rows_x[1], w_up[1, :, at], preferred_element_type=F32)
        gate, up = gate * inv_rms, up * inv_rms
        hidden[:, at] = (gate * jax.nn.sigmoid(gate) * up).astype(BF16)
        return carry

    lax.fori_loop(0, hid // tile, second, 0)

    for copy in down_in:
        copy.wait()
    pairs = []
    for d in range(zeds):
        z = lax.rem(zed + d + 1, zeds)
        pair_send[d] = jnp.dot(
            hidden[...],
            w_down[:, pl.ds(pl.multiple_of(z * width, width), width)],
            preferred_element_type=F32,
        ).astype(BF16)
        pairs.append(remote(pair_send.at[d], pair_recv.at[d], chan=partner))
    for copy in share_in:
        copy.wait()
    answers = []
    for d in range(zeds):
        z = lax.rem(zed + d + 1, zeds)
        mine = jnp.dot(
            hidden[...],
            w_share[:hid, pl.ds(pl.multiple_of(z * width, width), width)],
            preferred_element_type=F32,
        )
        pairs[d].wait_recv()
        ans_send[d] = (mine + pair_recv[d].astype(F32)).astype(BF16)
        back = []
        for e in range(1, groups):
            to = lax.rem(grp + e, groups)
            back.append(
                remote(
                    ans_send.at[d, pl.ds(pl.multiple_of(to * rows, rows), rows), :],
                    ans_recv.at[d, grp],
                    grp=to,
                )
            )
        ans_recv[d, grp] = ans_send[d, own_rows, :]
        answers.append(back)
    finals = []
    for d in range(zeds):
        z = lax.rem(zed + d + 1, zeds)
        for copy in answers[d]:
            copy.wait_recv()
        mixed = jnp.zeros((rows, width), F32)
        for w in range(groups):
            label = w // sharers
            coefficient = jnp.where(first_id == label, weight_first, 0.0) + jnp.where(
                second_id == label, weight_second, 0.0
            )
            mixed = mixed + coefficient * ans_recv[d, w].astype(F32)
        if d < zeds - 1:
            fin_send[d] = mixed.astype(BF16)
            finals.append(remote(fin_send.at[d], fin_recv.at[d], chan=2 * z + core))
    out = mid + mixed
    for d in range(zeds - 1):
        finals[d].wait_recv()
        out = out + fin_recv[d].astype(F32)
    layer_ref[...] = out.astype(BF16)
    for copy in sent:
        copy.wait_send()
    state_out.wait()


def per_device(
    residual,
    conv_input,
    gate_input,
    conv_state,
    conv_weight,
    conv_bias,
    state_proj,
    step_proj,
    step_bias,
    decay_rate,
    skip_gain,
    ssm_state,
    out_proj,
    router,
    expert_ids,
    expert_gate,
    expert_up,
    expert_down,
):
    rows, width = residual.shape
    groups = lax.axis_size("grp")
    chans = lax.axis_size("chan")
    zeds = chans // 2
    full = width * chans
    half = full // 2
    chn = conv_input.shape[1]
    hid = expert_gate.shape[2]
    experts = router.shape[1]
    rn = rows // chans
    allrows = rows * groups
    window = conv_state.astype(F32)
    convolved = (
        conv_weight[0] * window[:, 0]
        + conv_weight[1] * window[:, 1]
        + conv_weight[2] * window[:, 2]
        + conv_weight[3] * conv_input.astype(F32)
        + conv_bias
    )
    inner_act = jax.nn.silu(convolved).astype(BF16)
    router_wide = jnp.pad(router.astype(F32), ((0, 0), (0, 128 - experts)))
    padded = -(-state_proj.shape[1] // 128) * 128
    remotes = (
        2 * (chans - 1)
        + zeds
        + 2 * (zeds - 1)
        + zeds * (groups - 1)
        + (chans - 1)
        + (groups - 1)
        + 1
        + zeds
        + zeds * (groups - 1)
        + (zeds - 1)
    )
    locals_ = 2 + 8 * zeds
    scratch = [
        pltpu.VMEM((2, half, hid), BF16),
        pltpu.VMEM((2, half, hid), BF16),
        pltpu.VMEM((hid, half), BF16),
        pltpu.VMEM((max(2 * chn, hid), half), BF16),
        pltpu.VMEM(ssm_state.shape, F32),
        pltpu.VMEM((rows, padded), F32),
        pltpu.VMEM((chans, rn, padded), F32),
        pltpu.VMEM((chans, rn, padded), F32),
        pltpu.VMEM((chans, rn, padded), F32),
        pltpu.VMEM((rows, padded), F32),
        pltpu.VMEM((rows, chn), F32),
        pltpu.VMEM((rows, chn), F32),
        pltpu.VMEM((rows, chn), F32),
        pltpu.VMEM((zeds, rows, width), BF16),
        pltpu.VMEM((zeds, rows, width), BF16),
        pltpu.VMEM((zeds, rows, width), BF16),
        pltpu.VMEM((zeds, rows, width), BF16),
        pltpu.VMEM((2, allrows, half), BF16),
        pltpu.VMEM((rows, 128), F32),
        pltpu.VMEM((chans, rows, 128), F32),
        pltpu.VMEM((allrows, 128), F32),
        pltpu.VMEM((allrows, hid), F32),
        pltpu.VMEM((allrows, hid), F32),
        pltpu.VMEM((allrows, hid), BF16),
        pltpu.VMEM((zeds, allrows, width), BF16),
        pltpu.VMEM((zeds, allrows, width), BF16),
        pltpu.VMEM((zeds, allrows, width), BF16),
        pltpu.VMEM((zeds, groups, rows, width), BF16),
        pltpu.VMEM((zeds, rows, width), BF16),
        pltpu.VMEM((zeds, rows, width), BF16),
        pltpu.SemaphoreType.DMA((locals_,)),
        pltpu.SemaphoreType.DMA((remotes,)),
        pltpu.SemaphoreType.DMA((remotes,)),
    ]
    vmem = pl.BlockSpec(memory_space=pltpu.VMEM)
    anywhere = pl.BlockSpec(memory_space=pl.ANY)
    layer_out, new_state = pl.pallas_call(
        functools.partial(fused, chans, groups, experts),
        out_shape=(
            jax.ShapeDtypeStruct((rows, width), BF16),
            jax.ShapeDtypeStruct(ssm_state.shape, F32),
        ),
        in_specs=[vmem] * 10 + [anywhere] * 5,
        out_specs=(vmem, anywhere),
        scratch_shapes=scratch,
        compiler_params=pltpu.CompilerParams(
            collective_id=0,
            has_side_effects=True,
            vmem_limit_bytes=63 * 2**20,
        ),
        cost_estimate=pl.CostEstimate(
            flops=6 * allrows * full * hid,
            bytes_accessed=6 * full * hid,
            transcendentals=ssm_state.size,
        ),
    )(
        inner_act,
        residual,
        gate_input,
        state_proj,
        step_proj,
        step_bias.reshape(1, chn),
        decay_rate,
        skip_gain.reshape(1, chn),
        router_wide,
        expert_ids,
        ssm_state,
        out_proj,
        expert_gate,
        expert_up,
        expert_down,
    )
    return (layer_out, new_state)


def solution(mesh):
    return jax.shard_map(
        per_device,
        mesh=mesh,
        in_specs=(
            P("grp", "chan"),
            P("grp", "chan"),
            P("grp", "chan"),
            P("grp", None, "chan"),
            P(None, "chan"),
            P("chan"),
            P("chan", None),
            P(None, "chan"),
            P("chan"),
            P(None, "chan"),
            P("chan"),
            P("grp", None, "chan"),
            P("chan", None),
            P("chan", None),
            P("grp", None),
            P("grp", None, "chan"),
            P("grp", None, "chan"),
            P("grp", "chan", None),
        ),
        out_specs=(P("grp", "chan"), P("grp", None, "chan")),
        check_vma=False,
    )
```

time: 197 us -> 69.1 us (0.35)
  blocking collectives: 83.2 us -> 0 us
  Pallas kernels: 0 us -> 54.8 us
  waiting for transfers between devices: 50.3 us -> 0 us
  matrix products: 33.7 us -> 0 us
  between operations: 14.2 us -> 0.66 us
  local copies, waits for them, and re-layouts: 1.28 us -> 9.86 us
  other arithmetic: 10.4 us -> 3.27 us
  starting transfers between devices: 3.4 us -> 0 us
    psum x3 -> x0, blocking collectives: 58.8 us -> none  [the longest x1 30.7 us: per_device(): lax.psum(jnp.dot(inner_act, state_proj, preferred_element_type=jnp.float3...]
    pallas_call x0 -> x1, Pallas kernels: none -> 54.8 us  [per_device(): pl.pallas_call(functools.partial(fused, chans, groups, experts), out_shap...]
    reduce_scatter x2 -> x0, waiting for transfers between devices: 45.4 us -> none  [the longest x1 28.7 us: per_device(): lax.psum_scatter(lax.dot_general(columns, gated_out, (((0,), (1,)), ((),...]
    dot_general x8 -> x0, matrix products: 33.7 us -> none  [the longest x1 17.2 us: per_device(): lax.dot_general(columns, hidden, (((0,), (1,)), ((), ())), preferred_elem...]
    all_gather x1 -> x0, blocking collectives: 15.8 us -> none  [per_device(): lax.all_gather(incoming.reshape(groups * capacity, part_width), 'chan', a...]
    unnamed x13 -> x5, local copies, waits for them, and re-layouts: 0.12 us -> 8.98 us
    all_to_all x1 -> x0, blocking collectives: 8.62 us -> none  [per_device(): lax.all_to_all(copies, 'grp', split_axis=0, concat_axis=0, tiled=True)]
    reduce_sum x5 -> x0, other arithmetic: 5.04 us -> none  [the longest x1 3.78 us: per_device(): jnp.sum(output_mix[:, :, None] * new_state, axis=1) + skip_gain * inner_wide]
  transfers between devices with their start and end apart: 3 -> 0, of which waited for: 3 -> 0; matrix products, arithmetic and copies ran while one was open for 0% -> 0% of each run, Pallas kernels for 0% -> 0%
where the time goes in v1:
time: 69.1 us; the launch traced here: 68.6 us
  Pallas kernels  54.8 us (79%)
  local copies, waits for them, and re-layouts  9.86 us (14%)
  other arithmetic  3.27 us (5%)
    pallas_call x1, Pallas kernels, per_device(): pl.pallas_call(functools.partial(fused, chans, groups, experts), out_shap...  54.8 us
    unnamed x5, local copies, waits for them, and re-layouts  8.98 us
    convert_element_type x1, other arithmetic, per_device(): inner_act = jax.nn.silu(convolved).astype(BF16)  1.56 us

profile of v1, /device:TPU:0, one launch (start us, length us, event | category | flops | bytes accessed | tf_op | source)
XLA Modules:
  0.0 68.6 jit_solution(1266881637422750590)
XLA Ops:
  0.6 1.4 %copy.22.ids_ref = s32[32,2]{1,0:T(8,128)} copy(s32[32,2]{0,1:T(2,128)} %param.32) | data formatting | bytes 512 | tf_op args[14]
  2.0 0.9 %fusion.7 = (f32[1,1024]{1,0:T(1,128)S(1)}, f32[1,1024]{1,0:T(1,128)S(1)}, f32[1,1024]{1,0:T(1,128)S(1)}, f32[1,1024]{1,0:T(1,128)S(1)}) fusion(f32[4,1024]{1,0:T(4,128)} %param.22), kind=kLoop, calls=%fused_computation.12 | loop fusion | bytes 32768 | tf_op jit(solution)/shard_map/slice | solution.py:431
  2.9 0.9 %copy.20 = bf16[512,4]{1,0:T(8,128)(2,1)S(1)} copy(bf16[512,4]{0,1:T(4,128)(2,1)} %param.31) | data formatting | bytes 8192 | tf_op args[13]
  3.7 0.8 %pad_convert_fusion.router_ref = f32[512,128]{1,0:T(8,128)} fusion(bf16[512,4]{1,0:T(8,128)(2,1)S(1)} %copy.20), kind=kLoop, calls=%fused_computation.10 | loop fusion | flops 65536 | bytes 266240 | tf_op jit(solution)/shard_map/jit(_pad)/pad | solution.py:438
  4.5 1.0 %convert_element_type.12 = f32[32,3,1024]{2,0,1:T(8,128)S(1)} convert(bf16[32,3,1024]{2,0,1:T(8,128)(2,1)} %param.21) | non-fusion elementwise | flops 98304 | bytes 589824 | tf_op jit(solution)/shard_map/convert_element_type | solution.py:429
  5.5 1.6 %multiply_convert_fusion.inner_ref = bf16[32,1024]{1,0:T(8,128)(2,1)} fusion(f32[32,3,1024]{2,0,1:T(8,128)S(1)} %convert_element_type.12, bf16[32,1024]{1,0:T(8,128)(2,1)} %param.19, f32[1024]{0:T(1024)} %param.23, f32[1024]{0:T(1024)S(1)} %bitcast.38, f32[1024]{0:T(1024)S(1)} %bitcast.39, f32[1024]{0:T(1024)S(1)} %bitcast.37, f32[1024]{0:T(1024)S(1)} %bitcast.36), kind=kLoop, calls=%fused_computation.11 | loop fusion | flops 458752 | bytes 544768 | tf_op jit(solution)/shard_map/convert_element_type | solution.py:437
  7.0 2.2 %copy.21.state_proj_ref = bf16[1024,288]{1,0:T(8,128)(2,1)} copy(bf16[1024,288]{0,1:T(8,128)(2,1)} %param.24) | data formatting | bytes 1179648 | tf_op args[6]
  9.2 54.8 %shard_map.185 = (bf16[32,512]{1,0:T(8,128)(2,1)}, f32[32,16,1024]{2,1,0:T(8,128)}) custom-call(bf16[32,1024]{1,0:T(8,128)(2,1)} %multiply_convert_fusion.inner_ref, bf16[32,512]{1,0:T(8,128)(2,1)} %residual_ref.1, bf16[32,1024]{1,0:T(8,128)(2,1)} %gate_in_ref.1, bf16[1024,288]{1,0:T(8,128)(2,1)} %copy.21.state_proj_ref, bf16[256,1024]{1,0:T(8,128)(2,1)} %step_proj_ref.1, ...), custom_call_target="tpu_custom_call" | custom-call | flops 6442450944 | bytes 50331648 | tf_op jit(solution)/shard_map/pallas_call | solution.py:490
  64.1 1.4 %copy.25 = bf16[32,512]{1,0:T(8,128)(2,1)} copy(bf16[32,512]{1,0:T(8,128)(2,1)} %get-tuple-element.8) | data formatting | bytes 65536
  65.4 3.2 %copy.26 = f32[32,16,1024]{2,1,0:T(8,128)} copy(f32[32,16,1024]{2,1,0:T(8,128)} %get-tuple-element.9) | data formatting | bytes 4194304

commit v2 on v1

--- a/solution.py
+++ b/solution.py
@@ -16,7 +16,10 @@
     chans,
     groups,
     experts,
-    inner_ref,
+    conv_input_ref,
+    conv_state_ref,
+    conv_weight_ref,
+    conv_bias_ref,
     residual_ref,
     gate_in_ref,
     state_proj_ref,
@@ -77,7 +80,7 @@
     rows, width = residual_ref.shape
     full = width * chans
     half = full // 2
-    chn = inner_ref.shape[1]
+    chn = conv_input_ref.shape[1]
     rank = step_proj_ref.shape[0]
     nst = decay_ref.shape[0]
     hid = w_down.shape[0]
@@ -114,7 +117,44 @@
         parity = (1 - core) if other else core
         return pl.ds(pl.multiple_of((2 * z + parity) * width, width), width)
 
+    barrier = pltpu.get_barrier_semaphore()
+    for d in range(1, chans):
+        pl.semaphore_signal(
+            barrier,
+            inc=1,
+            device_id={"chan": lax.rem(me + d, chans)},
+            device_id_type=pl.DeviceIdType.MESH,
+        )
+    for d in range(1, groups):
+        pl.semaphore_signal(
+            barrier,
+            inc=1,
+            device_id={"grp": lax.rem(grp + d, groups)},
+            device_id_type=pl.DeviceIdType.MESH,
+        )
+
     state_in = local(ssm_hbm, state)
+
+    convolved = (
+        conv_weight_ref[0:1, :] * conv_state_ref[0].astype(F32)
+        + conv_weight_ref[1:2, :] * conv_state_ref[1].astype(F32)
+        + conv_weight_ref[2:3, :] * conv_state_ref[2].astype(F32)
+        + conv_weight_ref[3:4, :] * conv_input_ref[...].astype(F32)
+        + conv_bias_ref[...]
+    )
+    inner = (convolved * jax.nn.sigmoid(convolved)).astype(BF16)
+    padded = proj.shape[1]
+    partial[:, rank:] = jnp.zeros((rows, padded - rank), F32)
+    partial[:, : rank + 2 * nst] = lax.dot_general(
+        inner, state_proj_ref[...], (((1,), (1,)), ((), ())), preferred_element_type=F32
+    )
+    for j in range(chans):
+        proj_send[j] = partial[j * rn : (j + 1) * rn, :]
+    pl.semaphore_wait(barrier, chans - 1 + groups - 1)
+    arrivals = []
+    for d in range(1, chans):
+        to = lax.rem(me + d, chans)
+        arrivals.append(remote(proj_send.at[to], proj_recv.at[d], chan=to))
     mixer_in = [
         local(
             out_proj_hbm.at[:, columns(z, p == 0)],
@@ -137,36 +177,6 @@
         local(down_hbm.at[0, :, columns(z, True)], w_down.at[:, pl.ds(z * width, width)])
         for z in range(zeds)
     ]
-
-    barrier = pltpu.get_barrier_semaphore()
-    for d in range(1, chans):
-        pl.semaphore_signal(
-            barrier,
-            inc=1,
-            device_id={"chan": lax.rem(me + d, chans)},
-            device_id_type=pl.DeviceIdType.MESH,
-        )
-    for d in range(1, groups):
-        pl.semaphore_signal(
-            barrier,
-            inc=1,
-            device_id={"grp": lax.rem(grp + d, groups)},
-            device_id_type=pl.DeviceIdType.MESH,
-        )
-
-    inner = inner_ref[...]
-    padded = proj.shape[1]
-    partial[:, rank:] = jnp.zeros((rows, padded - rank), F32)
-    partial[:, : rank + 2 * nst] = jnp.dot(
-        inner, state_proj_ref[...], preferred_element_type=F32
-    )
-    for j in range(chans):
-        proj_send[j] = partial[j * rn : (j + 1) * rn, :]
-    pl.semaphore_wait(barrier, chans - 1 + groups - 1)
-    arrivals = []
-    for d in range(1, chans):
-        to = lax.rem(me + d, chans)
-        arrivals.append(remote(proj_send.at[to], proj_recv.at[d], chan=to))
     total = proj_send[me]
     for d in range(1, chans):
         arrivals[d - 1].wait_recv()
@@ -177,6 +187,11 @@
         to = lax.rem(me + d, chans)
         arrivals.append(remote(proj_all.at[me], proj_all.at[me], chan=to))
     inner_wide = inner.astype(F32)
+    router_wide = jnp.concatenate(
+        [router_ref[...].astype(F32), jnp.zeros((128 - experts, width), F32)], axis=0
+    )
+    ids = jnp.concatenate([ids_ref[...].astype(F32), jnp.zeros((126, rows), F32)], axis=0).T
+    first_id, second_id = ids[:, 0:1].astype(jnp.int32), ids[:, 1:2].astype(jnp.int32)
     gate_in = gate_in_ref[...].astype(F32)
     for copy in arrivals:
         copy.wait_recv()
@@ -262,14 +277,16 @@
         if d:
             over_z[d - 1].wait_recv()
         z = lax.rem(zed + zeds - d, zeds)
-        for e in range(1, groups):
-            over_grp.append(remote(cell(z), cell(z), grp=lax.rem(grp + e, groups)))
+        over_grp.append(
+            [remote(cell(z), cell(z), grp=lax.rem(grp + e, groups)) for e in range(1, groups)]
+        )
         if d == 0:
             lane = lax.broadcasted_iota(jnp.int32, (rows, 128), 1)
             squares = jnp.sum(mid * mid, axis=1, keepdims=True)
-            scores = jnp.dot(
+            scores = lax.dot_general(
                 mid,
-                router_ref[...],
+                router_wide,
+                (((1,), (1,)), ((), ())),
                 precision=lax.Precision.HIGHEST,
                 preferred_element_type=F32,
             )
@@ -278,6 +295,35 @@
             for c in range(1, chans):
                 to = lax.rem(me + c, chans)
                 stats.append(remote(stat_own, stat_recv.at[c], chan=to))
+
+    tile = min(1024, hid)
+    for copy in expert_in[0]:
+        copy.wait()
+    across = []
+
+    def own_half(d):
+        z = lax.rem(zed + zeds - d, zeds)
+        part = pl.ds(pl.multiple_of(z * width, width), width)
+        for copy in over_grp[d]:
+            copy.wait_recv()
+        across.append(
+            remote(rows_x.at[0, :, part], rows_x.at[1, :, part], chan=partner)
+        )
+
+        def first(n, carry):
+            at = pl.ds(pl.multiple_of(n * tile, tile), tile)
+            gate = jnp.dot(rows_x[0, :, part], w_gate[0, part, at], preferred_element_type=F32)
+            up = jnp.dot(rows_x[0, :, part], w_up[0, part, at], preferred_element_type=F32)
+            if d:
+                gate, up = gate + acc_gate[:, at], up + acc_up[:, at]
+            acc_gate[:, at] = gate
+            acc_up[:, at] = up
+            return carry
+
+        lax.fori_loop(0, hid // tile, first, 0)
+
+    for d in range(zeds // 2):
+        own_half(d)
     summary = stat_own[...]
     for c in range(1, chans):
         stats[c - 1].wait_recv()
@@ -292,25 +338,11 @@
                 grp=lax.rem(grp + e, groups),
             )
         )
-    for copy in over_grp:
-        copy.wait_recv()
-    across = remote(rows_x.at[0], rows_x.at[1], chan=partner)
-
-    tile = min(256, hid)
-    for copy in expert_in[0]:
-        copy.wait()
-
-    def first(n, carry):
-        at = pl.ds(pl.multiple_of(n * tile, tile), tile)
-        acc_gate[:, at] = jnp.dot(rows_x[0], w_gate[0, :, at], preferred_element_type=F32)
-        acc_up[:, at] = jnp.dot(rows_x[0], w_up[0, :, at], preferred_element_type=F32)
-        return carry
-
-    lax.fori_loop(0, hid // tile, first, 0)
+    for d in range(zeds // 2, zeds):
+        own_half(d)
 
     scale = lax.rsqrt(summary[:, experts : experts + 1] / full + EPSILON)
     logits = summary * scale
-    first_id, second_id = ids_ref[:, 0:1], ids_ref[:, 1:2]
     chosen_first = jnp.sum(jnp.where(lane == first_id, logits, 0.0), axis=1, keepdims=True)
     chosen_second = jnp.sum(jnp.where(lane == second_id, logits, 0.0), axis=1, keepdims=True)
     weight_first = jax.nn.sigmoid(chosen_first - chosen_second)
@@ -321,7 +353,8 @@
     inv_rms = lax.rsqrt(stat_all[:, experts : experts + 1] / full + EPSILON)
     for copy in expert_in[1]:
         copy.wait()
-    across.wait_recv()
+    for copy in across:
+        copy.wait_recv()
 
     def second(n, carry):
         at = pl.ds(pl.multiple_of(n * tile, tile), tile)
@@ -338,7 +371,8 @@
     for copy in down_in:
         copy.wait()
     pairs = []
-    for d in range(zeds):
+
+    def other_half(d):
         z = lax.rem(zed + d + 1, zeds)
         pair_send[d] = jnp.dot(
             hidden[...],
@@ -346,10 +380,14 @@
             preferred_element_type=F32,
         ).astype(BF16)
         pairs.append(remote(pair_send.at[d], pair_recv.at[d], chan=partner))
+
+    other_half(0)
     for copy in share_in:
         copy.wait()
     answers = []
     for d in range(zeds):
+        if d < zeds - 1:
+            other_half(d + 1)
         z = lax.rem(zed + d + 1, zeds)
         mine = jnp.dot(
             hidden[...],
@@ -395,6 +433,29 @@
     state_out.wait()
 
 
+def deliver(layer_in, state_in, layer_out, state_out, layer_buf, state_buf, in_sem, out_sem):
+    parts = in_sem.shape[0] - 1
+    count = state_buf.shape[0] // parts
+    pieces = [
+        (state_in.at[at], state_buf.at[at], state_out.at[at])
+        for at in [pl.ds(p * count, count) for p in range(parts)]
+    ]
+    pieces.append((layer_in, layer_buf, layer_out))
+    incoming = [
+        pltpu.make_async_copy(src, buf, in_sem.at[k]) for k, (src, buf, _) in enumerate(pieces)
+    ]
+    outgoing = [
+        pltpu.make_async_copy(buf, dst, out_sem.at[k]) for k, (_, buf, dst) in enumerate(pieces)
+    ]
+    for copy in incoming:
+        copy.start()
+    for arrived, leaving in zip(incoming, outgoing):
+        arrived.wait()
+        leaving.start()
+    for copy in outgoing:
+        copy.wait()
+
+
 def per_device(
     residual,
     conv_input,
@@ -426,16 +487,6 @@
     experts = router.shape[1]
     rn = rows // chans
     allrows = rows * groups
-    window = conv_state.astype(F32)
-    convolved = (
-        conv_weight[0] * window[:, 0]
-        + conv_weight[1] * window[:, 1]
-        + conv_weight[2] * window[:, 2]
-        + conv_weight[3] * conv_input.astype(F32)
-        + conv_bias
-    )
-    inner_act = jax.nn.silu(convolved).astype(BF16)
-    router_wide = jnp.pad(router.astype(F32), ((0, 0), (0, 128 - experts)))
     padded = -(-state_proj.shape[1] // 128) * 128
     remotes = (
         2 * (chans - 1)
@@ -444,7 +495,7 @@
         + zeds * (groups - 1)
         + (chans - 1)
         + (groups - 1)
-        + 1
+        + zeds
         + zeds
         + zeds * (groups - 1)
         + (zeds - 1)
@@ -493,7 +544,7 @@
             jax.ShapeDtypeStruct((rows, width), BF16),
             jax.ShapeDtypeStruct(ssm_state.shape, F32),
         ),
-        in_specs=[vmem] * 10 + [anywhere] * 5,
+        in_specs=[vmem] * 13 + [anywhere] * 5,
         out_specs=(vmem, anywhere),
         scratch_shapes=scratch,
         compiler_params=pltpu.CompilerParams(
@@ -507,23 +558,42 @@
             transcendentals=ssm_state.size,
         ),
     )(
-        inner_act,
+        conv_input,
+        conv_state.transpose(1, 0, 2),
+        conv_weight,
+        conv_bias.reshape(1, chn),
         residual,
         gate_input,
-        state_proj,
+        state_proj.T,
         step_proj,
         step_bias.reshape(1, chn),
         decay_rate,
         skip_gain.reshape(1, chn),
-        router_wide,
-        expert_ids,
+        router.T,
+        expert_ids.T,
         ssm_state,
         out_proj,
         expert_gate,
         expert_up,
         expert_down,
     )
-    return (layer_out, new_state)
+    return tuple(
+        pl.pallas_call(
+            deliver,
+            out_shape=(
+                jax.ShapeDtypeStruct((rows, width), BF16),
+                jax.ShapeDtypeStruct(ssm_state.shape, F32),
+            ),
+            in_specs=[anywhere] * 2,
+            out_specs=(anywhere, anywhere),
+            scratch_shapes=[
+                pltpu.VMEM((rows, width), BF16),
+                pltpu.VMEM(ssm_state.shape, F32),
+                pltpu.SemaphoreType.DMA((9,)),
+                pltpu.SemaphoreType.DMA((9,)),
+            ],
+        )(layer_out, new_state)
+    )
 
 
 def solution(mesh):

time: 69.1 us -> 54.1 us (0.78)
  local copies, waits for them, and re-layouts: 9.86 us -> 0 us
  other arithmetic: 3.27 us -> 0 us
  Pallas kernels: 54.8 us -> 53.2 us
    unnamed x5 -> x0, local copies, waits for them, and re-layouts: 8.98 us -> none
    pallas_call x1, Pallas kernels: 54.8 us -> 50.8 us  [per_device(): pl.pallas_call(functools.partial(fused, chans, groups, experts), out_shap...]
    convert_element_type x2 -> x0, other arithmetic: 2.51 us -> none  [the longest x1 1.56 us: per_device(): inner_act = jax.nn.silu(convolved).astype(BF16)]
    pallas_call x0 -> x1, Pallas kernels: none -> 2.41 us  [per_device(): pl.pallas_call(deliver, out_shape=(jax.ShapeDtypeStruct((rows, width), BF...]
    slice x1 -> x0, local copies, waits for them, and re-layouts: 0.88 us -> none  [per_device(): conv_weight[0] * window[:, 0] + conv_weight[1] * window[:, 1]]
    pad x1 -> x0, other arithmetic: 0.76 us -> none  [per_device(): router_wide = jnp.pad(router.astype(F32), ((0, 0), (0, 128 - experts)))]
where the time goes in v2:
time: 54.1 us; the launch traced here: 53.9 us
  Pallas kernels  53.2 us (98%)
  between operations  0.65 us (1%)
    pallas_call x1, Pallas kernels, per_device(): pl.pallas_call(functools.partial(fused, chans, groups, experts), out_shap...  50.8 us
    pallas_call x1, Pallas kernels, per_device(): pl.pallas_call(deliver, out_shape=(jax.ShapeDtypeStruct((rows, width), BF...  2.41 us

profile of v2, /device:TPU:0, one launch (start us, length us, event | category | flops | bytes accessed | tf_op | source)
XLA Modules:
  0.0 53.9 jit_solution(6308971305040911226)
XLA Ops:
  0.6 50.8 %shard_map.185 = (bf16[32,512]{1,0:T(8,128)(2,1)}, f32[32,16,1024]{2,1,0:T(8,128)}) custom-call(bf16[32,1024]{1,0:T(8,128)(2,1)} %conv_input_ref.1, bf16[3,32,1024]{2,1,0:T(8,128)(2,1)} %bitcast.8, f32[4,1024]{1,0:T(4,128)} %conv_weight_ref.1, f32[1,1024]{1,0:T(1,128)} %bitcast.9, bf16[32,512]{1,0:T(8,128)(2,1)} %residual_ref.1, ...), custom_call_target="tpu_custom_call" | custom-call | flops 6442450944 | bytes 50331648 | tf_op jit(solution)/shard_map/pallas_call | solution.py:541
  51.5 2.4 %shard_map.186 = (bf16[32,512]{1,0:T(8,128)(2,1)}, f32[32,16,1024]{2,1,0:T(8,128)}) custom-call(bf16[32,512]{1,0:T(8,128)(2,1)} %get-tuple-element.4.layer_in, f32[32,16,1024]{2,1,0:T(8,128)} %get-tuple-element.5.state_in), custom_call_target="tpu_custom_call" | custom-call | tf_op jit(solution)/shard_map/pallas_call | solution.py:581
